TPU v7x, 32 devices: a whole 2x2x4 slice. The times are simulated.
32 devices in a mesh: rep: 2 (over y), wide: 4 (over z), tp: 4 (over x, core).
Axes of the slice: x: 2, y: 2, z: 4, core: 2. Of those that a mesh axis runs over, the one named last changes fastest.
Arguments:
- tokens: bfloat16 [256, 8192], P(('rep', 'wide'), 'tp'), parts along dimension 0, may hold values from -6 to 6
- adapter_ids: int32 [256], P(('rep', 'wide')), parts along dimension 0, may hold values from 0 to 3, as said below
- adapter_slot: int32 [4], replicated, may hold values from 0 to 3, each once
- gate_weight: bfloat16 [8192, 28672], P('tp', 'wide'), may hold values from -127 to 127
- up_weight: bfloat16 [8192, 28672], P('tp', 'wide'), may hold values from -127 to 127
- hidden_unit_scales: float32 [2, 28672], P(None, 'wide'), may hold values from 7e-05 to 0.0003
- shrink_weight: bfloat16 [4, 8192, 128], P('wide', 'tp'), may hold values from -0.0625 to 0.0625
- expand_weight: bfloat16 [4, 2, 64, 28672], P('tp', None, None, 'wide'), may hold values from -0.75 to 0.75
Outputs:
- hidden: bfloat16 [256, 28672], P(('rep', 'tp'), 'wide'), parts along dimension 0
There are 2 independent parts, one for each index of `rep`. A program takes and returns all parts, laid end to end along the dimension named above; an argument that names none is the same for every part. Nothing has to cross between parts.
Inputs may be any that keep to these rules, and one draw needn't show every extreme that they name: `adapter_ids`: within the rows of one index of wide (aligned blocks of 32 rows) no adapter is named more than 16 times; in every block one adapter, the same one for all blocks of a part, is named exactly 16 times. `adapter_slot`: each slot holds one adapter.
All inputs are finite; a program needn't handle non-finite values.
Results may differ from a plain program's by a relative error of at most 0.015.
Values may be sent and summed in bfloat16 or wider, within the bound.
A program may use at most 192 MiB of HBM per device.

v0:
```python
import jax
import jax.numpy as jnp
from jax import lax
from jax.sharding import PartitionSpec as P

adapter_gain = 0.5


def lookup_slots(table, wanted):
    matches = wanted[:, None] == jnp.arange(table.shape[0], dtype=jnp.int32)[None, :]
    return jnp.sum(jnp.where(matches, table[None, :], 0), axis=1)


def shards(
    tokens,
    adapter_ids,
    adapter_slot,
    gate_weight,
    up_weight,
    hidden_unit_scales,
    shrink_weight,
    expand_weight,
):
    row_dev, feature_part = tokens.shape
    wide_index = lax.axis_index("wide")
    rank_double = shrink_weight.shape[2]
    rank_size = rank_double // 2
    tokens_all, ids_all = (
        lax.all_gather(tokens, "wide", axis=0, tiled=True),
        lax.all_gather(adapter_ids, "wide", axis=0, tiled=True),
    )
    rows_total = tokens_all.shape[0]
    slot_all = lookup_slots(adapter_slot, ids_all)
    slot_dev = lax.dynamic_slice_in_dim(slot_all, wide_index * row_dev, row_dev, 0)
    shard_piece = lax.all_gather(shrink_weight, "wide", axis=0, tiled=True)
    products = jnp.einsum("rd,jdk->rjk", tokens, shard_piece, preferred_element_type=jnp.float32)
    picked = slot_dev[:, None] == jnp.arange(shard_piece.shape[0], dtype=jnp.int32)[None, :]
    shrink_part = jnp.sum(jnp.where(picked[:, :, None], products, 0.0), axis=1)
    shrink_dev = lax.psum(shrink_part, "tp").astype(jnp.bfloat16)
    shrink_all = lax.all_gather(shrink_dev, "wide", axis=0, tiled=True)
    resident_count = expand_weight.shape[0]
    columns = expand_weight.shape[3]
    first_local = lax.axis_index("tp") * resident_count
    chosen = (
        slot_all[:, None] == first_local + jnp.arange(resident_count, dtype=jnp.int32)[None, :]
    ).astype(jnp.bfloat16)
    gate_input_rows = (chosen[:, :, None] * shrink_all[:, None, :rank_size]).reshape(
        rows_total, resident_count * rank_size
    )
    up_input_rows = (chosen[:, :, None] * shrink_all[:, None, rank_size:]).reshape(
        rows_total, resident_count * rank_size
    )
    expand_gate = expand_weight[:, 0].reshape(resident_count * rank_size, columns)
    up_expansion = expand_weight[:, 1].reshape(resident_count * rank_size, columns)
    gate_adapter_term = jnp.dot(
        tokens_all, gate_weight, preferred_element_type=jnp.float32
    ) * hidden_unit_scales[0] + adapter_gain * jnp.dot(
        gate_input_rows, expand_gate, preferred_element_type=jnp.float32
    )
    up_adapter_term = jnp.dot(
        tokens_all, up_weight, preferred_element_type=jnp.float32
    ) * hidden_unit_scales[1] + adapter_gain * jnp.dot(
        up_input_rows, up_expansion, preferred_element_type=jnp.float32
    )
    summed = lax.psum_scatter(
        jnp.stack([gate_adapter_term, up_adapter_term], axis=1).astype(jnp.bfloat16),
        "tp",
        scatter_dimension=0,
        tiled=True,
    ).astype(jnp.float32)
    return (jax.nn.silu(summed[:, 0]) * summed[:, 1]).astype(jnp.bfloat16)


def solution(mesh):
    return jax.shard_map(
        shards,
        mesh=mesh,
        in_specs=(
            P(("rep", "wide"), "tp"),
            P(("rep", "wide")),
            P(),
            P("tp", "wide"),
            P("tp", "wide"),
            P(None, "wide"),
            P("wide", "tp", None),
            P("tp", None, None, "wide"),
        ),
        out_specs=P(("rep", "tp"), "wide"),
        check_vma=False,
    )
```

profile of v0, /device:TPU:0, one launch (start us, length us, event | category | flops | bytes accessed | tf_op | source)
XLA Modules:
  0.0 155.2 jit_solution(10910376596274563297)
XLA Ops:
  6.5 0.0 all-gather.2.cloned.1.call-start
  6.5 0.7 all-gather.2.cloned.1.call-update
  7.3 0.0 reduce-scatter.2.cloned.1.call-start
  7.3 1.2 dynamic-slice
  9.2 0.9 dynamic-update-slice
  10.1 9.9 %all-reduce = s32[128]{0:T(128)S(1)} all-reduce(s32[128]{0:T(128)S(1)} %dynamic-update-slice), channel_id=1, replica_groups=mesh['rep'=2,'wide'=4,'tp'=4] {'wide'}, use_global_device_ids=true, to_apply=%add | all-reduce | flops 128 | bytes 1024
  20.0 0.7 select_reduce_fusion
  20.7 0.1 dynamic_slice.3
  20.8 0.9 fusion.16
  21.7 21.4 %all_gather.12 = bf16[128,2048]{1,0:T(8,128)(2,1)S(1)} all-gather(bf16[32,2048]{1,0:T(8,128)(2,1)} %param.8), channel_id=1, replica_groups=mesh['rep'=2,'wide'=4,'tp'=4] {'wide'}, dimensions={0}, use_global_device_ids=true | all-gather | bytes 655360 | tf_op jit(solution)/shard_map/all_gather | solution.py:29
  43.1 15.3 %convolution_multiply_fusion.1 = f32[128,7168]{1,0:T(8,128)} fusion(bf16[128,2048]{1,0:T(8,128)(2,1)S(1)} %all_gather.12, bf16[2048,7168]{1,0:T(8,128)(2,1)} %param.12, f32[7168]{0:T(1024)S(1)} %bitcast.32), kind=kOutput, calls=%fused_computation.2 | convolution fusion | flops 3759013888 | bytes 33583104 | tf_op jit(solution)/shard_map/dot_general | solution.py:60
  58.4 0.0 copy-start.2
  58.4 0.0 copy-start.1
  58.4 15.3 %convolution_multiply_fusion.3 = f32[128,7168]{1,0:T(8,128)} fusion(bf16[128,2048]{1,0:T(8,128)(2,1)S(1)} %all_gather.12, bf16[2048,7168]{1,0:T(8,128)(2,1)} %param.11, f32[7168]{0:T(1024)S(1)} %bitcast.31), kind=kOutput, calls=%fused_computation.5 | convolution fusion | flops 3759013888 | bytes 33583104 | tf_op jit(solution)/shard_map/dot_general | solution.py:55
  73.7 0.0 all-gather.2.cloned.1.call-done
  73.7 0.0 copy-done.2
  73.7 2.1 %fusion.6 = f32[32,128]{1,0:T(8,128)S(1)} fusion(bf16[4,2048,128]{2,1,0:T(8,128)(2,1)} %all-gather.2.cloned.1.call-done, bf16[32,2048]{1,0:T(8,128)(2,1)S(1)} %copy-done.2, pred[32,4]{0,1:T(4,128)(4,1)S(1)} %iota_compare_fusion), kind=kOutput, calls=%fused_computation.12 | convolution fusion | flops 67137536 | bytes 2244736 | tf_op jit(solution)/shard_map/rd,jdk->rjk/dot_general | solution.py:36
  75.8 10.1 %psum.7 = bf16[32,128]{1,0:T(8,128)(2,1)S(1)} all-reduce(f32[32,128]{1,0:T(8,128)S(1)} %fusion.6), channel_id=1, replica_groups=mesh['rep'=2,'wide'=4,'tp'=4] {'tp'}, use_global_device_ids=true, to_apply=%region_2.3 | all-reduce | flops 4096 | bytes 24576 | tf_op jit(solution)/shard_map/psum | solution.py:39
  85.9 0.0 copy-start
  85.9 13.2 %all_gather.15 = bf16[128,128]{1,0:T(8,128)(2,1)S(1)} all-gather(bf16[32,128]{1,0:T(8,128)(2,1)S(1)} %psum.7), channel_id=1, replica_groups=mesh['rep'=2,'wide'=4,'tp'=4] {'wide'}, dimensions={0}, use_global_device_ids=true | all-gather | bytes 40960 | tf_op jit(solution)/shard_map/all_gather | solution.py:40
  99.1 0.0 copy-done.1
  99.1 2.7 %fusion.4 = bf16[128,1,7168]{2,0,1:T(8,128)(2,1)S(1)} fusion(f32[128,7168]{1,0:T(8,128)} %convolution_multiply_fusion.1, bf16[1,2,64,7168]{3,2,1,0:T(8,128)(2,1)S(1)} %copy-done.1, bf16[128,128]{1,0:T(8,128)(2,1)S(1)} %all_gather.15, bf16[128]{0:T(256)(128)(2,1)S(1)} %compare_convert_fusion), kind=kOutput, calls=%fused_computation.8 | convolution fusion | flops 120201216 | bytes 6455808 | tf_op jit(solution)/shard_map/dot_general | solution.py:62
  101.9 0.0 copy-done
  101.9 0.7 fusion.5
  102.6 2.1 %pad_maximum_fusion = bf16[128,2,7168]{2,0,1:T(8,128)(2,1)} fusion(bf16[128,1,7168]{2,0,1:T(8,128)(2,1)S(1)} %fusion.4, bf16[128,1,7168]{2,0,1:T(8,128)(2,1)S(1)} %fusion.5), kind=kLoop, calls=%fused_computation.10 | loop fusion | flops 1835008 | bytes 7340032 | tf_op jit(solution)/shard_map/stack | solution.py:66
  104.7 0.0 reduce-scatter.2.cloned.1.call-update
  104.7 41.3 %reduce-scatter.2.cloned.1.call-done = bf16[32,2,7168]{2,0,1:T(8,128)(2,1)} async-done(((bf16[128,2,7168]{2,0,1:T(8,128)(2,1)}), bf16[32,2,7168]{2,0,1:T(8,128)(2,1)}) %reduce-scatter.2.cloned.1.call-update) | async-done | bytes 917520 | tf_op jit(solution)/shard_map/reduce_scatter | solution.py:65
  146.0 1.3 convert_element_type.21
  147.3 1.0 fusion.8
  (3 shorter events, 0.0 us)
Async XLA Ops:
  6.5 67.2 %all-gather.2.cloned.1.call-start = ((), (), s32[]{:S(2)}) async-start(), calls=%async_computation.1 | async-start | bytes 2621440 | tf_op jit(solution)/shard_map/all_gather | solution.py:35
  7.3 138.8 %reduce-scatter.2.cloned.1.call-start = ((), (), s32[]{:S(2)}) async-start(), calls=%async_computation.2 | async-start | bytes 4587520 | tf_op jit(solution)/shard_map/reduce_scatter | solution.py:65
  58.4 15.3 %copy-start.2 = (bf16[32,2048]{1,0:T(8,128)(2,1)S(1)}, bf16[32,2048]{1,0:T(8,128)(2,1)}, u32[]{:S(2)}) copy-start(bf16[32,2048]{1,0:T(8,128)(2,1)} %param.8) | copy-start | bytes 393220
  58.4 40.7 %copy-start.1 = (bf16[1,2,64,7168]{3,2,1,0:T(8,128)(2,1)S(1)}, bf16[1,2,64,7168]{3,2,1,0:T(8,128)(2,1)}, u32[]{:S(2)}) copy-start(bf16[1,2,64,7168]{3,2,1,0:T(8,128)(2,1)} %param.15) | copy-start | bytes 5505028
  85.9 16.0 %copy-start = (f32[128,7168]{1,0:T(8,128)S(1)}, f32[128,7168]{1,0:T(8,128)}, u32[]{:S(2)}) copy-start(f32[128,7168]{1,0:T(8,128)} %convolution_multiply_fusion.3) | copy-start | bytes 11010052
Sparse Core Ops, SparseCore 0:
  8.9 56.9 all-gather.1
  104.8 41.1 reduce-scatter.1
where the time goes:
time: 156 us; the launch traced here: 155 us
  blocking collectives  54.7 us (35%)
  waiting for transfers between devices  42 us (27%)
  matrix products  36 us (23%)
  between operations  14.1 us (9%)
  other arithmetic  5.19 us (3%)
  local copies, waits for them, and re-layouts  3.13 us (2%)
    reduce_scatter x1, waiting for transfers between devices, shards(): lax.psum_scatter(jnp.stack([gate_adapter_term, up_adapter_term], axis=1)....  41.3 us
    all_gather x1, blocking collectives, shards(): lax.all_gather(tokens, 'wide', axis=0, tiled=True)  21.4 us
    dot_general x1, matrix products, shards(): jnp.dot(tokens_all, gate_weight, preferred_element_type=jnp.float32)  15.3 us
    dot_general x1, matrix products, shards(): jnp.dot(tokens_all, up_weight, preferred_element_type=jnp.float32)  15.3 us
    all_gather x1, blocking collectives, shards(): shrink_all = lax.all_gather(shrink_dev, 'wide', axis=0, tiled=True)  13.2 us
    psum x1, blocking collectives, shards(): shrink_dev = lax.psum(shrink_part, 'tp').astype(jnp.bfloat16)  10.1 us
    unnamed x1, blocking collectives  9.89 us
  transfers between devices with their start and end apart: 2, of which 1 were waited for; matrix products, arithmetic and copies ran while one was open for 22% of the time, Pallas kernels for 0%

commit v1 on v0

v1 whole, which is shorter than its diff:
```python
import functools

import jax
import jax.numpy as jnp
from jax import lax
from jax.experimental import pallas as pl
from jax.experimental.pallas import tpu as pltpu
from jax.sharding import PartitionSpec as P

adapter_gain = 0.5
lag = 1
weight_bytes = 40 * 2**20
MESH = pl.DeviceIdType.MESH


def fused(
    nw,
    nt,
    bufs,
    tokens,
    slots,
    gate_weight,
    up_weight,
    scales,
    shrink_weight,
    expand_weight,
    out,
    tok_all,
    slot_all,
    wbuf,
    ebuf,
    scale_buf,
    shrink_buf,
    part,
    part_recv,
    low,
    sel,
    term,
    recv1,
    send2,
    recv2,
    w_sem,
    misc_sem,
    tok_send,
    tok_recv,
    part_send_sem,
    part_recv_sem,
    low_send_sem,
    low_recv_sem,
    s1_send,
    s1_recv,
    s2_send,
    s2_recv,
):
    row_dev = tokens.shape[0]
    slots_wide = shrink_weight.shape[0]
    slots_tp = expand_weight.shape[0]
    rank = expand_weight.shape[2]
    sources = slots_tp // slots_wide
    tiles, _, nh, _, row_tp, cb = term.shape
    wide = lax.axis_index("wide")
    tp = lax.axis_index("tp")
    lo = lax.rem(tp, 2)
    hi = lax.div(tp, 2)

    def columns(i):
        return pl.ds(pl.multiple_of(i * cb, cb), cb)

    def weight_copies(i, slot):
        return [
            pltpu.make_async_copy(w.at[:, columns(i)], wbuf.at[slot, p], w_sem.at[slot, p])
            for p, w in enumerate((gate_weight, up_weight))
        ]

    own_rows = pl.ds(pl.multiple_of(wide * row_dev, row_dev), row_dev)
    local = [
        pltpu.make_async_copy(tokens, tok_all.at[own_rows], misc_sem.at[0]),
        pltpu.make_async_copy(slots, slot_all.at[own_rows], misc_sem.at[1]),
        pltpu.make_async_copy(shrink_weight, shrink_buf, misc_sem.at[2]),
        pltpu.make_async_copy(scales, scale_buf, misc_sem.at[3]),
        pltpu.make_async_copy(expand_weight, ebuf, misc_sem.at[4]),
    ]

    barrier = pltpu.get_barrier_semaphore()
    for d in range(1, nw):
        pl.semaphore_signal(
            barrier, inc=1, device_id={"wide": lax.rem(wide + d, nw)}, device_id_type=MESH
        )
    for d in range(1, nt):
        pl.semaphore_signal(
            barrier, inc=1, device_id={"tp": lax.rem(tp + d, nt)}, device_id_type=MESH
        )
    for copy in local:
        copy.start()
    for i in range(bufs):
        for copy in weight_copies(i, i):
            copy.start()
    pl.semaphore_wait(barrier, nw + nt - 2)

    def token_copies(d):
        there = {"wide": lax.rem(wide + d, nw)}
        return [
            pltpu.make_async_remote_copy(
                src_ref=src,
                dst_ref=dst.at[own_rows],
                send_sem=tok_send.at[d - 1, k],
                recv_sem=tok_recv.at[d - 1, k],
                device_id=there,
                device_id_type=MESH,
            )
            for k, (src, dst) in enumerate(((tokens, tok_all), (slots, slot_all)))
        ]

    gather = [token_copies(d) for d in range(1, nw)]
    for pair in gather:
        for copy in pair:
            copy.start()
    for copy in local:
        copy.wait()
    for pair in gather:
        for copy in pair:
            copy.wait()

    total = None
    for j in range(slots_wide):
        product = jnp.dot(tok_all[...], shrink_buf[j], preferred_element_type=jnp.float32)
        product = jnp.where(slot_all[...] == wide * slots_wide + j, product, 0.0)
        total = product if total is None else total + product
    part[...] = total

    owner = lax.div(wide, sources)
    ahead = lax.rem(owner - tp + nt, nt)

    def part_copy(d):
        return pltpu.make_async_remote_copy(
            src_ref=part,
            dst_ref=part_recv.at[d - 1],
            send_sem=part_send_sem,
            recv_sem=part_recv_sem.at[d - 1],
            device_id={"tp": owner},
            device_id_type=MESH,
        )

    for d in range(1, nt):

        @pl.when(ahead == d)
        def _():
            part_copy(d).start()

    def low_copy(d, j):
        return pltpu.make_async_remote_copy(
            src_ref=low.at[j],
            dst_ref=low.at[j],
            send_sem=low_send_sem.at[d - 1],
            recv_sem=low_recv_sem.at[j],
            device_id={"wide": lax.rem(wide + d, nw)},
            device_id_type=MESH,
        )

    own_source = lax.rem(wide, sources)

    @pl.when(ahead == 0)
    def _():
        value = part[...]
        for d in range(1, nt):
            part_copy(d).wait_recv()
            value = value + part_recv[d - 1]
        low[own_source] = value.astype(jnp.bfloat16)
        for d in range(1, nw):
            low_copy(d, own_source).start()

    for j in range(sources):

        @pl.when(wide != tp * sources + j)
        def _():
            low_copy(1, j).wait_recv()

    for j in range(slots_tp):
        chosen = jnp.where(
            slot_all[...] == tp * slots_tp + j, low[j // slots_wide].astype(jnp.float32), 0.0
        ).astype(jnp.bfloat16)
        for p in range(2):
            sel[p, :, j * rank : (j + 1) * rank] = chosen[:, p * rank : (p + 1) * rank]

    for d in range(1, nt):

        @pl.when(ahead == d)
        def _():
            part_copy(d).wait_send()

    @pl.when(ahead == 0)
    def _():
        for d in range(1, nw):
            low_copy(d, own_source).wait_send()

    def first_copy(i):
        return pltpu.make_async_remote_copy(
            src_ref=term.at[i, 1 - lo],
            dst_ref=recv1.at[i],
            send_sem=s1_send.at[i],
            recv_sem=s1_recv.at[i],
            device_id={"tp": 2 * hi + 1 - lo},
            device_id_type=MESH,
        )

    def second_copy(i, d):
        return pltpu.make_async_remote_copy(
            src_ref=send2.at[i, d - 1],
            dst_ref=recv2.at[i, d - 1],
            send_sem=s2_send.at[i, d - 1],
            recv_sem=s2_recv.at[i, d - 1],
            device_id={"tp": 2 * lax.rem(hi + d, nh) + lo},
            device_id_type=MESH,
        )

    def exchange(i):
        first_copy(i).wait_recv()
        for d in range(1, nh):
            h = lax.rem(hi + d, nh)
            send2[i, d - 1] = (
                term[i, lo, h].astype(jnp.float32) + recv1[i, h].astype(jnp.float32)
            ).astype(jnp.bfloat16)
            second_copy(i, d).start()

    def tile(i, carry):
        slot = lax.rem(i, bufs)
        for copy in weight_copies(i, slot):
            copy.wait()
        for p in range(2):
            main = jnp.dot(tok_all[...], wbuf[slot, p], preferred_element_type=jnp.float32)
            e = ebuf[:, p, :, columns(i)].reshape(slots_tp * rank, cb)
            low_term = jnp.dot(sel[p], e, preferred_element_type=jnp.float32)
            value = main * scale_buf[pl.ds(p, 1), columns(i)] + adapter_gain * low_term
            value = value.astype(jnp.bfloat16)
            for t in range(nt):
                term[i, t % 2, t // 2, p] = value[t * row_tp : (t + 1) * row_tp]
        first_copy(i).start()

        @pl.when(i + bufs < tiles)
        def _():
            for copy in weight_copies(i + bufs, slot):
                copy.start()

        @pl.when(i >= lag)
        def _():
            exchange(i - lag)

        return carry

    lax.fori_loop(0, tiles, tile, 0)
    for i in range(max(tiles - lag, 0), tiles):
        exchange(i)

    def finish(i, carry):
        sums = []
        for d in range(1, nh):
            second_copy(i, d).wait_recv()
        for p in range(2):
            value = term[i, lo, hi, p].astype(jnp.float32) + recv1[i, hi, p].astype(jnp.float32)
            for d in range(1, nh):
                value = value + recv2[i, d - 1, p].astype(jnp.float32)
            sums.append(value)
        gate, up = sums
        out[:, columns(i)] = (gate / (1.0 + jnp.exp(-gate)) * up).astype(jnp.bfloat16)
        return carry

    lax.fori_loop(0, tiles, finish, 0)

    def drain(i, carry):
        first_copy(i).wait_send()
        for d in range(1, nh):
            second_copy(i, d).wait_send()
        return carry

    lax.fori_loop(0, tiles, drain, 0)


def shards(
    nw,
    nt,
    tokens,
    adapter_ids,
    adapter_slot,
    gate_weight,
    up_weight,
    hidden_unit_scales,
    shrink_weight,
    expand_weight,
):
    row_dev, features = tokens.shape
    columns = gate_weight.shape[1]
    rows = row_dev * nw
    row_tp = rows // nt
    nh = nt // 2
    slots_tp, _, rank, _ = expand_weight.shape
    slots_wide = shrink_weight.shape[0]
    sources = slots_tp // slots_wide
    cb = max(c for c in (128, 256, 512) if columns % c == 0)
    tiles = columns // cb
    bufs = max(1, min(tiles, weight_bytes // (features * cb * 4)))

    matches = adapter_ids[:, None] == jnp.arange(adapter_slot.shape[0], dtype=jnp.int32)[None, :]
    slot = jnp.sum(jnp.where(matches, adapter_slot[None, :], 0), axis=1)
    slots = jnp.broadcast_to(slot[:, None], (row_dev, 2 * rank))

    bf16, f32 = jnp.bfloat16, jnp.float32
    DMA = pltpu.SemaphoreType.DMA
    return pl.pallas_call(
        functools.partial(fused, nw, nt, bufs),
        out_shape=jax.ShapeDtypeStruct((row_tp, columns), bf16),
        in_specs=[pl.BlockSpec(memory_space=pl.ANY)] * 7,
        out_specs=pl.BlockSpec(memory_space=pltpu.VMEM),
        scratch_shapes=[
            pltpu.VMEM((rows, features), bf16),
            pltpu.VMEM((rows, 2 * rank), jnp.int32),
            pltpu.VMEM((bufs, 2, features, cb), bf16),
            pltpu.VMEM(expand_weight.shape, bf16),
            pltpu.VMEM((2, columns), f32),
            pltpu.VMEM(shrink_weight.shape, bf16),
            pltpu.VMEM((rows, 2 * rank), f32),
            pltpu.VMEM((nt - 1, rows, 2 * rank), f32),
            pltpu.VMEM((sources, rows, 2 * rank), bf16),
            pltpu.VMEM((2, rows, slots_tp * rank), bf16),
            pltpu.VMEM((tiles, 2, nh, 2, row_tp, cb), bf16),
            pltpu.VMEM((tiles, nh, 2, row_tp, cb), bf16),
            pltpu.VMEM((tiles, nh - 1, 2, row_tp, cb), bf16),
            pltpu.VMEM((tiles, nh - 1, 2, row_tp, cb), bf16),
            DMA((bufs, 2)),
            DMA((5,)),
            DMA((nw - 1, 2)),
            DMA((nw - 1, 2)),
            DMA,
            DMA((nt - 1,)),
            DMA((nw - 1,)),
            DMA((sources,)),
            DMA((tiles,)),
            DMA((tiles,)),
            DMA((tiles, nh - 1)),
            DMA((tiles, nh - 1)),
        ],
        compiler_params=pltpu.CompilerParams(
            collective_id=0, has_side_effects=True, vmem_limit_bytes=60 * 2**20
        ),
        cost_estimate=pl.CostEstimate(
            flops=4 * rows * features * columns,
            bytes_accessed=4 * features * columns,
            transcendentals=row_tp * columns,
        ),
    )(
        tokens,
        slots,
        gate_weight,
        up_weight,
        hidden_unit_scales,
        shrink_weight,
        expand_weight,
    )


def solution(mesh):
    return jax.shard_map(
        functools.partial(shards, mesh.shape["wide"], mesh.shape["tp"]),
        mesh=mesh,
        in_specs=(
            P(("rep", "wide"), "tp"),
            P(("rep", "wide")),
            P(),
            P("tp", "wide"),
            P("tp", "wide"),
            P(None, "wide"),
            P("wide", "tp", None),
            P("tp", None, None, "wide"),
        ),
        out_specs=P(("rep", "tp"), "wide"),
        check_vma=False,
    )
```

time: 156 us -> 54.1 us (0.35)
  blocking collectives: 54.7 us -> 0 us
  Pallas kernels: 0 us -> 50.7 us
  waiting for transfers between devices: 42 us -> 0 us
  matrix products: 36 us -> 0 us
  between operations: 14.1 us -> 0.01 us
  other arithmetic: 5.19 us -> 0.75 us
    pallas_call x0 -> x1, Pallas kernels: none -> 50.7 us  [shards(): pl.pallas_call(functools.partial(fused, nw, nt, bufs), out_shape=jax.Shap...]
    reduce_scatter x1 -> x0, waiting for transfers between devices: 41.3 us -> none  [shards(): lax.psum_scatter(jnp.stack([gate_adapter_term, up_adapter_term], axis=1)....]
    dot_general x5 -> x0, matrix products: 36 us -> none  [the longest x1 15.3 us: shards(): jnp.dot(tokens_all, gate_weight, preferred_element_type=jnp.float32)]
    all_gather x2 -> x0, blocking collectives: 34.6 us -> none  [the longest x1 21.4 us: shards(): lax.all_gather(tokens, 'wide', axis=0, tiled=True)]
    psum x1 -> x0, blocking collectives: 10.1 us -> none  [shards(): shrink_dev = lax.psum(shrink_part, 'tp').astype(jnp.bfloat16)]
    unnamed x1 -> x0, blocking collectives: 9.89 us -> none
    convert_element_type x3 -> x0, other arithmetic: 2.32 us -> none  [the longest x1 1.3 us: shards(): summed = lax.psum_scatter(jnp.stack([gate_adapter_term, up_adapter_term],...]
    another operation x1 -> x0, other arithmetic: 2.11 us -> none  [shards(): jnp.stack([gate_adapter_term, up_adapter_term], axis=1).astype(jnp.bfloat16)]
  transfers between devices with their start and end apart: 2 -> 0, of which waited for: 1 -> 0; matrix products, arithmetic and copies ran while one was open for 22% -> 0% of each run, Pallas kernels for 0% -> 0%
where the time goes in v1:
time: 54.1 us; the launch traced here: 54 us
  Pallas kernels  50.7 us (94%)
  local copies, waits for them, and re-layouts  2.49 us (5%)
  other arithmetic  0.75 us (1%)
    pallas_call x1, Pallas kernels, shards(): pl.pallas_call(functools.partial(fused, nw, nt, bufs), out_shape=jax.Shap...  50.7 us
    unnamed x1, local copies, waits for them, and re-layouts  1.82 us

profile of v1, /device:TPU:0, one launch (start us, length us, event | category | flops | bytes accessed | tf_op | source)
XLA Modules:
  0.0 54.0 jit_solution(3022051279052143671)
XLA Ops:
  0.0 0.8 %select_reduce_fusion = s32[32]{0:T(128)S(1)} fusion(s32[4]{0:T(128)} %param.10, s32[32]{0:T(128)} %param.9), kind=kLoop, calls=%fused_computation | loop fusion | flops 352 | bytes 272 | tf_op jit(solution)/shard_map/reduce_sum | solution.py:303
  0.8 0.7 %broadcast_in_dim.23.slots = s32[32,128]{1,0:T(8,128)} broadcast(s32[32]{0:T(128)S(1)} %select_reduce_fusion), dimensions={0} | broadcast | bytes 16512 | tf_op jit(solution)/shard_map/broadcast_in_dim | solution.py:304
  1.4 50.7 %shard_map.82 = bf16[32,7168]{1,0:T(8,128)(2,1)} custom-call(bf16[32,2048]{1,0:T(8,128)(2,1)} %tokens.1, s32[32,128]{1,0:T(8,128)} %broadcast_in_dim.23.slots, bf16[2048,7168]{1,0:T(8,128)(2,1)} %gate_weight.1, bf16[2048,7168]{1,0:T(8,128)(2,1)} %up_weight.1, f32[2,7168]{1,0:T(2,128)} %scales.1, bf16[1,2048,128]{2,1,0:T(8,128)(2,1)} %shrink_weight.1, ...), custom_call_target="tpu_custom_call" | custom-call | flops 7516192768 | bytes 58720256 | tf_op jit(solution)/shard_map/pallas_call | solution.py:308
  52.2 1.8 %copy.10 = bf16[32,7168]{1,0:T(8,128)(2,1)} copy(bf16[32,7168]{1,0:T(8,128)(2,1)} %shard_map.82) | data formatting | bytes 917504

commit v2 on v1

--- a/solution.py
+++ b/solution.py
@@ -9,6 +9,7 @@
 
 adapter_gain = 0.5
 lag = 1
+early = 3
 weight_bytes = 40 * 2**20
 MESH = pl.DeviceIdType.MESH
 
@@ -18,7 +19,8 @@
     nt,
     bufs,
     tokens,
-    slots,
+    ids,
+    table,
     gate_weight,
     up_weight,
     scales,
@@ -26,6 +28,8 @@
     expand_weight,
     out,
     tok_all,
+    slot_own,
+    slot_rows,
     slot_all,
     wbuf,
     ebuf,
@@ -35,6 +39,7 @@
     part_recv,
     low,
     sel,
+    acc,
     term,
     recv1,
     send2,
@@ -43,6 +48,8 @@
     misc_sem,
     tok_send,
     tok_recv,
+    slot_send,
+    slot_recv,
     part_send_sem,
     part_recv_sem,
     low_send_sem,
@@ -75,10 +82,9 @@
     own_rows = pl.ds(pl.multiple_of(wide * row_dev, row_dev), row_dev)
     local = [
         pltpu.make_async_copy(tokens, tok_all.at[own_rows], misc_sem.at[0]),
-        pltpu.make_async_copy(slots, slot_all.at[own_rows], misc_sem.at[1]),
-        pltpu.make_async_copy(shrink_weight, shrink_buf, misc_sem.at[2]),
-        pltpu.make_async_copy(scales, scale_buf, misc_sem.at[3]),
-        pltpu.make_async_copy(expand_weight, ebuf, misc_sem.at[4]),
+        pltpu.make_async_copy(shrink_weight, shrink_buf, misc_sem.at[1]),
+        pltpu.make_async_copy(scales, scale_buf, misc_sem.at[2]),
+        pltpu.make_async_copy(expand_weight, ebuf, misc_sem.at[3]),
     ]
 
     barrier = pltpu.get_barrier_semaphore()
@@ -97,36 +103,51 @@
             copy.start()
     pl.semaphore_wait(barrier, nw + nt - 2)
 
-    def token_copies(d):
-        there = {"wide": lax.rem(wide + d, nw)}
-        return [
-            pltpu.make_async_remote_copy(
-                src_ref=src,
-                dst_ref=dst.at[own_rows],
-                send_sem=tok_send.at[d - 1, k],
-                recv_sem=tok_recv.at[d - 1, k],
-                device_id=there,
-                device_id_type=MESH,
-            )
-            for k, (src, dst) in enumerate(((tokens, tok_all), (slots, slot_all)))
-        ]
-
-    gather = [token_copies(d) for d in range(1, nw)]
-    for pair in gather:
-        for copy in pair:
-            copy.start()
+    def token_copy(d):
+        return pltpu.make_async_remote_copy(
+            src_ref=tokens,
+            dst_ref=tok_all.at[own_rows],
+            send_sem=tok_send.at[d - 1],
+            recv_sem=tok_recv.at[d - 1],
+            device_id={"wide": lax.rem(wide + d, nw)},
+            device_id_type=MESH,
+        )
+
+    slot_row = jnp.zeros(ids.shape, jnp.float32)
+    for a in range(table.shape[1]):
+        slot_row = jnp.where(ids[...] == a, table[0, a].astype(jnp.float32), slot_row)
+    slot_own[...] = jnp.zeros_like(slot_own)
+    slot_own[0:1, 0:row_dev] = slot_row
+    slot_rows[wide] = slot_own[...]
+
+    def slot_copy(d):
+        return pltpu.make_async_remote_copy(
+            src_ref=slot_own,
+            dst_ref=slot_rows.at[wide],
+            send_sem=slot_send.at[d - 1],
+            recv_sem=slot_recv.at[d - 1],
+            device_id={"wide": lax.rem(wide + d, nw)},
+            device_id_type=MESH,
+        )
+
+    for d in range(1, nw):
+        slot_copy(d).start()
+
+    for d in range(1, nw):
+        token_copy(d).start()
     for copy in local:
         copy.wait()
-    for pair in gather:
-        for copy in pair:
-            copy.wait()
-
-    total = None
-    for j in range(slots_wide):
-        product = jnp.dot(tok_all[...], shrink_buf[j], preferred_element_type=jnp.float32)
-        product = jnp.where(slot_all[...] == wide * slots_wide + j, product, 0.0)
-        total = product if total is None else total + product
-    part[...] = total
+    for d in range(1, nw):
+        slot_copy(d).wait()
+    diagonal = lax.broadcasted_iota(jnp.int32, (row_dev, row_dev), 0) == lax.broadcasted_iota(
+        jnp.int32, (row_dev, row_dev), 1
+    )
+    for b in range(nw):
+        row = jnp.broadcast_to(slot_rows[b, 0:1, 0:row_dev], (row_dev, row_dev))
+        column = jnp.sum(jnp.where(diagonal, row, 0.0), axis=1, keepdims=True)
+        slot_all[b * row_dev : (b + 1) * row_dev, :] = jnp.broadcast_to(
+            column, (row_dev, slot_all.shape[1])
+        )
 
     owner = lax.div(wide, sources)
     ahead = lax.rem(owner - tp + nt, nt)
@@ -141,6 +162,16 @@
             device_id_type=MESH,
         )
 
+    for d in range(1, nw):
+        token_copy(d).wait()
+
+    total = None
+    for j in range(slots_wide):
+        product = jnp.dot(tok_all[...], shrink_buf[j], preferred_element_type=jnp.float32)
+        mine = slot_all[...] == (wide * slots_wide + j).astype(jnp.float32)
+        product = jnp.where(mine, product, 0.0)
+        total = product if total is None else total + product
+    part[...] = total
     for d in range(1, nt):
 
         @pl.when(ahead == d)
@@ -169,6 +200,27 @@
         for d in range(1, nw):
             low_copy(d, own_source).start()
 
+    def main_term(i, p):
+        main = jnp.dot(
+            tok_all[...], wbuf[lax.rem(i, bufs), p], preferred_element_type=jnp.float32
+        )
+        return main * scale_buf[pl.ds(p, 1), columns(i)]
+
+    def begin(i, carry):
+        for p, copy in enumerate(weight_copies(i, lax.rem(i, bufs))):
+            copy.wait()
+            acc[i, p] = main_term(i, p)
+
+        @pl.when(i + bufs < tiles)
+        def _():
+            for copy in weight_copies(i + bufs, lax.rem(i, bufs)):
+                copy.start()
+
+        return carry
+
+    ahead_tiles = acc.shape[0]
+    lax.fori_loop(0, ahead_tiles, begin, 0)
+
     for j in range(sources):
 
         @pl.when(wide != tp * sources + j)
@@ -177,7 +229,7 @@
 
     for j in range(slots_tp):
         chosen = jnp.where(
-            slot_all[...] == tp * slots_tp + j, low[j // slots_wide].astype(jnp.float32), 0.0
+            slot_all[...] == (tp * slots_tp + j).astype(jnp.float32), low[j // slots_wide].astype(jnp.float32), 0.0
         ).astype(jnp.bfloat16)
         for p in range(2):
             sel[p, :, j * rank : (j + 1) * rank] = chosen[:, p * rank : (p + 1) * rank]
@@ -222,18 +274,31 @@
             ).astype(jnp.bfloat16)
             second_copy(i, d).start()
 
+    def send_term(i, p, main):
+        e = ebuf[:, p, :, columns(i)].reshape(slots_tp * rank, cb)
+        low_term = jnp.dot(sel[p], e, preferred_element_type=jnp.float32)
+        value = (main + adapter_gain * low_term).astype(jnp.bfloat16)
+        for t in range(nt):
+            term[i, t % 2, t // 2, p] = value[t * row_tp : (t + 1) * row_tp]
+
+    def complete(i, carry):
+        for p in range(2):
+            send_term(i, p, acc[i, p])
+        first_copy(i).start()
+
+        @pl.when(i >= lag)
+        def _():
+            exchange(i - lag)
+
+        return carry
+
+    lax.fori_loop(0, ahead_tiles, complete, 0)
+
     def tile(i, carry):
         slot = lax.rem(i, bufs)
-        for copy in weight_copies(i, slot):
+        for p, copy in enumerate(weight_copies(i, slot)):
             copy.wait()
-        for p in range(2):
-            main = jnp.dot(tok_all[...], wbuf[slot, p], preferred_element_type=jnp.float32)
-            e = ebuf[:, p, :, columns(i)].reshape(slots_tp * rank, cb)
-            low_term = jnp.dot(sel[p], e, preferred_element_type=jnp.float32)
-            value = main * scale_buf[pl.ds(p, 1), columns(i)] + adapter_gain * low_term
-            value = value.astype(jnp.bfloat16)
-            for t in range(nt):
-                term[i, t % 2, t // 2, p] = value[t * row_tp : (t + 1) * row_tp]
+            send_term(i, p, main_term(i, p))
         first_copy(i).start()
 
         @pl.when(i + bufs < tiles)
@@ -241,13 +306,10 @@
             for copy in weight_copies(i + bufs, slot):
                 copy.start()
 
-        @pl.when(i >= lag)
-        def _():
-            exchange(i - lag)
-
+        exchange(i - lag)
         return carry
 
-    lax.fori_loop(0, tiles, tile, 0)
+    lax.fori_loop(ahead_tiles, tiles, tile, 0)
     for i in range(max(tiles - lag, 0), tiles):
         exchange(i)
 
@@ -299,20 +361,25 @@
     tiles = columns // cb
     bufs = max(1, min(tiles, weight_bytes // (features * cb * 4)))
 
-    matches = adapter_ids[:, None] == jnp.arange(adapter_slot.shape[0], dtype=jnp.int32)[None, :]
-    slot = jnp.sum(jnp.where(matches, adapter_slot[None, :], 0), axis=1)
-    slots = jnp.broadcast_to(slot[:, None], (row_dev, 2 * rank))
-
+    ahead_tiles = max(lag, min(early, bufs, tiles))
+    slot_lanes = -(-row_dev // 128) * 128
     bf16, f32 = jnp.bfloat16, jnp.float32
     DMA = pltpu.SemaphoreType.DMA
     return pl.pallas_call(
         functools.partial(fused, nw, nt, bufs),
         out_shape=jax.ShapeDtypeStruct((row_tp, columns), bf16),
-        in_specs=[pl.BlockSpec(memory_space=pl.ANY)] * 7,
+        in_specs=[
+            pl.BlockSpec(memory_space=pl.ANY),
+            pl.BlockSpec(memory_space=pltpu.VMEM),
+            pl.BlockSpec(memory_space=pltpu.SMEM),
+        ]
+        + [pl.BlockSpec(memory_space=pl.ANY)] * 5,
         out_specs=pl.BlockSpec(memory_space=pltpu.VMEM),
         scratch_shapes=[
             pltpu.VMEM((rows, features), bf16),
-            pltpu.VMEM((rows, 2 * rank), jnp.int32),
+            pltpu.VMEM((8, slot_lanes), f32),
+            pltpu.VMEM((nw, 8, slot_lanes), f32),
+            pltpu.VMEM((rows, 2 * rank), f32),
             pltpu.VMEM((bufs, 2, features, cb), bf16),
             pltpu.VMEM(expand_weight.shape, bf16),
             pltpu.VMEM((2, columns), f32),
@@ -321,14 +388,17 @@
             pltpu.VMEM((nt - 1, rows, 2 * rank), f32),
             pltpu.VMEM((sources, rows, 2 * rank), bf16),
             pltpu.VMEM((2, rows, slots_tp * rank), bf16),
+            pltpu.VMEM((ahead_tiles, 2, rows, cb), f32),
             pltpu.VMEM((tiles, 2, nh, 2, row_tp, cb), bf16),
             pltpu.VMEM((tiles, nh, 2, row_tp, cb), bf16),
             pltpu.VMEM((tiles, nh - 1, 2, row_tp, cb), bf16),
             pltpu.VMEM((tiles, nh - 1, 2, row_tp, cb), bf16),
             DMA((bufs, 2)),
-            DMA((5,)),
-            DMA((nw - 1, 2)),
-            DMA((nw - 1, 2)),
+            DMA((4,)),
+            DMA((nw - 1,)),
+            DMA((nw - 1,)),
+            DMA((nw - 1,)),
+            DMA((nw - 1,)),
             DMA,
             DMA((nt - 1,)),
             DMA((nw - 1,)),
@@ -348,7 +418,8 @@
         ),
     )(
         tokens,
-        slots,
+        adapter_ids.reshape(1, row_dev),
+        adapter_slot.reshape(1, -1),
         gate_weight,
         up_weight,
         hidden_unit_scales,

time: 54.1 us -> 51.2 us (0.946)
  Pallas kernels: 50.7 us -> 49.2 us
  other arithmetic: 0.75 us -> 0 us
  local copies, waits for them, and re-layouts: 2.49 us -> 1.82 us
    pallas_call x1, Pallas kernels: 50.7 us -> 49.2 us  [shards(): pl.pallas_call(functools.partial(fused, nw, nt, bufs), out_shape=jax.Shap...]
    reduce_sum x1 -> x0, other arithmetic: 0.75 us -> none  [shards(): slot = jnp.sum(jnp.where(matches, adapter_slot[None, :], 0), axis=1)]
    broadcast_in_dim x1 -> x0, local copies, waits for them, and re-layouts: 0.68 us -> none  [shards(): slots = jnp.broadcast_to(slot[:, None], (row_dev, 2 * rank))]
where the time goes in v2:
time: 51.2 us; the launch traced here: 51.1 us
  Pallas kernels  49.2 us (96%)
  local copies, waits for them, and re-layouts  1.82 us (4%)
    pallas_call x1, Pallas kernels, shards(): pl.pallas_call(functools.partial(fused, nw, nt, bufs), out_shape=jax.Shap...  49.2 us
    unnamed x1, local copies, waits for them, and re-layouts  1.82 us

profile of v2, /device:TPU:0, one launch (start us, length us, event | category | flops | bytes accessed | tf_op | source)
XLA Modules:
  0.0 51.1 jit_solution(9312047248617398012)
XLA Ops:
  0.0 49.2 %shard_map.82 = bf16[32,7168]{1,0:T(8,128)(2,1)} custom-call(bf16[32,2048]{1,0:T(8,128)(2,1)} %tokens.1, s32[1,32]{1,0:T(1,128)} %bitcast.2, s32[1,4]{1,0:T(1,128)} %bitcast.3, bf16[2048,7168]{1,0:T(8,128)(2,1)} %gate_weight.1, bf16[2048,7168]{1,0:T(8,128)(2,1)} %up_weight.1, f32[2,7168]{1,0:T(2,128)} %scales.1, bf16[1,2048,128]{2,1,0:T(8,128)(2,1)} %shrink_weight.1, ...), custom_call_target="tpu_custom_call" | custom-call | flops 7516192768 | bytes 58720256 | tf_op jit(solution)/shard_map/pallas_call | solution.py:368
  49.2 1.8 %copy.10 = bf16[32,7168]{1,0:T(8,128)(2,1)} copy(bf16[32,7168]{1,0:T(8,128)(2,1)} %shard_map.82) | data formatting | bytes 917504
